TPU v7x, 256 devices: a whole 4x4x8 slice. The times are simulated.
256 devices in a mesh: expert: 64 (over z, x, core), replica: 4 (over y).
Axes of the slice: x: 4, y: 4, z: 8, core: 2. Of those that a mesh axis runs over, the one named last changes fastest.
Arguments:
- tokens: bfloat16 [49152, 3584], P(('expert', 'replica')), may hold values from -6 to 6
- routes: int32 [49152], P(('expert', 'replica')), may hold values from 0 to 64, as said below
- combine_weights: float32 [49152], P(('expert', 'replica')), may hold values from 0.2 to 1
- up_weight: bfloat16 [64, 3584, 1024], P('expert', None, 'replica'), may hold values from -0.09375 to 0.09375
- down_weight: bfloat16 [64, 1024, 3584], P('expert', 'replica'), may hold values from -0.1875 to 0.1875
- cotangent: bfloat16 [49152, 3584], P(('expert', 'replica')), may hold values from -6 to 6
Outputs:
- mixed: bfloat16 [49152, 3584], P(('expert', 'replica'))
- token_grads: bfloat16 [49152, 3584], P(('expert', 'replica'))
- combine_grads: float32 [49152], P(('expert', 'replica'))
- up_grads: bfloat16 [64, 3584, 1024], P('expert', None, 'replica')
- down_grads: bfloat16 [64, 1024, 3584], P('expert', 'replica')
Inputs may be any that keep to these rules, and one draw needn't show every extreme that they name: Among the 192 tokens of one device (aligned blocks of routes), no expert is named more than 3 times, and in every block some expert (not necessarily the same one in every block) is named exactly 3 times.
All inputs are finite; a program needn't handle non-finite values.
Results may differ from a plain program's by a relative error of at most 0.015.
Values may be sent and summed in bfloat16 or wider, within the bound.
A program may use at most 128 MiB of HBM per device.

v0:
```python
import jax
import jax.numpy as jnp
from jax import lax
from jax.sharding import PartitionSpec as P

CAP = 3


def slot_layout(routes, experts):
    token_count = routes.shape[0]
    labels = jnp.arange(experts, dtype=jnp.int32)
    onehot = (routes[:, None] == labels[None, :]).astype(jnp.int32)
    slot_rank = jnp.sum((jnp.cumsum(onehot, axis=0) - onehot) * onehot, axis=1)
    slot_of = jnp.where(routes < experts, routes * CAP + slot_rank, experts * CAP)
    slot_owner = jnp.full((experts * CAP + 1,), token_count, jnp.int32)
    slot_owner = slot_owner.at[slot_of].set(jnp.arange(token_count, dtype=jnp.int32))[
        : experts * CAP
    ]
    filled = slot_owner < token_count
    safe_index = jnp.where(filled, slot_owner, 0)
    return (slot_of, filled, safe_index)


def silu_slope(pre_act):
    sigmoid_value = jax.nn.sigmoid(pre_act)
    return sigmoid_value * (1.0 + pre_act * (1.0 - sigmoid_value))


def to_tokens(returned, slot_of):
    model_width = returned.shape[-1]
    flat_rows = returned.reshape(-1, model_width)
    padded = jnp.concatenate([flat_rows, jnp.zeros((1, model_width), flat_rows.dtype)], axis=0)
    return padded[slot_of]


def body(tokens, routes, combine_weights, up_weight, down_weight, cotangent):
    experts = lax.axis_size("expert")
    groups = lax.axis_size("replica")
    model_width = tokens.shape[1]
    contract_last = (((1,), (1,)), ((), ()))
    contract_first = (((0,), (0,)), ((), ()))
    slot_of, filled, safe_index = slot_layout(routes, experts)
    keep = filled[:, None]
    send_tokens = jnp.where(keep, tokens[safe_index], jnp.zeros((), tokens.dtype))
    arrived = lax.all_to_all(
        send_tokens.reshape(experts, CAP, model_width),
        "expert",
        split_axis=0,
        concat_axis=0,
        tiled=True,
    )
    arrived = arrived.reshape(experts * CAP, model_width)
    per_rows = arrived.shape[0]
    up_local = up_weight[0]
    down_local = down_weight[0]
    up_full, down_full = (
        lax.all_gather(up_local, "replica", axis=1, tiled=True),
        lax.all_gather(down_local, "replica", axis=0, tiled=True),
    )
    pre_act = jnp.dot(arrived, up_full, preferred_element_type=jnp.float32)
    hidden = jax.nn.silu(pre_act).astype(jnp.bfloat16)
    hidden_blocks = hidden.reshape(per_rows, groups, -1)
    down_blocks = down_full.reshape(groups, -1, model_width)
    out_parts = jnp.einsum(
        "rkf,kfd->krd", hidden_blocks, down_blocks, preferred_element_type=jnp.float32
    ).astype(jnp.bfloat16)
    expert_out = jnp.sum(out_parts.astype(jnp.float32), axis=0).astype(jnp.bfloat16)
    returned = lax.all_to_all(
        expert_out.reshape(experts, CAP, model_width),
        "expert",
        split_axis=0,
        concat_axis=0,
        tiled=True,
    )
    token_out = to_tokens(returned, slot_of)
    weights_col = combine_weights[:, None]
    mixed = (weights_col * token_out.astype(jnp.float32)).astype(jnp.bfloat16)
    combine_grads = jnp.sum(token_out.astype(jnp.float32) * cotangent.astype(jnp.float32), axis=1)
    scaled = combine_weights[safe_index][:, None] * cotangent[safe_index].astype(jnp.float32)
    send_grads = jnp.where(keep, scaled, jnp.zeros((), jnp.float32)).astype(jnp.bfloat16)
    out_grad = lax.all_to_all(
        send_grads.reshape(experts, CAP, model_width),
        "expert",
        split_axis=0,
        concat_axis=0,
        tiled=True,
    )
    out_grad = out_grad.reshape(per_rows, model_width)
    hidden_grad = lax.dot_general(
        out_grad, down_full, contract_last, preferred_element_type=jnp.float32
    )
    pre_grad = (hidden_grad * silu_slope(pre_act)).astype(jnp.bfloat16)
    down_grads = lax.psum_scatter(
        lax.dot_general(
            hidden, out_grad, contract_first, preferred_element_type=jnp.float32
        ).astype(jnp.bfloat16),
        "replica",
        scatter_dimension=0,
        tiled=True,
    )
    up_term = lax.dot_general(arrived, pre_grad, contract_first, preferred_element_type=jnp.float32)
    up_grads = lax.psum_scatter(
        up_term.astype(jnp.bfloat16), "replica", scatter_dimension=1, tiled=True
    )
    pre_blocks = pre_grad.reshape(per_rows, groups, -1)
    up_blocks = up_full.reshape(model_width, groups, -1)
    row_parts = jnp.einsum(
        "rkf,dkf->krd", pre_blocks, up_blocks, preferred_element_type=jnp.float32
    ).astype(jnp.bfloat16)
    row_grads = jnp.sum(row_parts.astype(jnp.float32), axis=0).astype(jnp.bfloat16)
    returned_grads = lax.all_to_all(
        row_grads.reshape(experts, CAP, model_width),
        "expert",
        split_axis=0,
        concat_axis=0,
        tiled=True,
    )
    token_rows = to_tokens(returned_grads, slot_of)
    token_grads = (weights_col * token_rows.astype(jnp.float32)).astype(jnp.bfloat16)
    return (mixed, token_grads, combine_grads, up_grads[None], down_grads[None])


def solution(mesh):
    return jax.shard_map(
        body,
        mesh=mesh,
        in_specs=(
            P(("expert", "replica"), None),
            P(("expert", "replica")),
            P(("expert", "replica")),
            P("expert", None, "replica"),
            P("expert", "replica", None),
            P(("expert", "replica"), None),
        ),
        out_specs=(
            P(("expert", "replica"), None),
            P(("expert", "replica"), None),
            P(("expert", "replica")),
            P("expert", None, "replica"),
            P("expert", "replica", None),
        ),
        check_vma=False,
    )
```

profile of v0, /device:TPU:1, one launch (start us, length us, event | category | flops | bytes accessed | tf_op | source)
XLA Modules:
  0.0 343.6 jit_solution(3457427335323402219)
XLA Ops:
  7.2 0.0 copy-start
  7.2 0.0 all-gather.5.cloned.1.call-start
  7.2 3.9 %copy.15 = bf16[1,3584,256]{1,2,0:T(8,128)(2,1)} copy(bf16[1,3584,256]{2,1,0:T(8,128)(2,1)} %param.9) | data formatting | bytes 3670016 | tf_op args[3]
  11.1 0.0 copy-start.5
  11.1 0.0 copy-start.3
  11.1 0.0 all-gather.5.cloned.1.call-update
  11.2 0.0 all-gather.7.cloned.1.call-start
  11.2 0.7 all-gather.7.cloned.1.call-update
  11.9 0.0 copy-done.5
  12.0 0.6 reduce-window.6
  12.6 0.2 slice_reduce_fusion
  12.8 0.1 bitcast_bitcast_fusion
  13.0 1.2 scatter_custom_fusion
  14.2 0.0 copy-done.3
  14.2 2.5 gather_fusion.3
  16.7 0.0 copy-start.2
  16.7 4.5 %reshape.91 = f32[64,3,3584]{2,1,0:T(4,128)} reshape(bf16[192,3584]{1,0:T(8,128)(2,1)} %gather_fusion.3) | data formatting | bytes 4128768 | tf_op jit(solution)/shard_map/convert_element_type | solution.py:79
  21.2 0.0 copy-done.2
  21.2 1.6 gather_fusion.2
  22.8 0.1 mul.56
  23.0 0.2 lt.27
  23.1 4.6 %select_convert_fusion = bf16[64,3,3584]{2,1,0:T(4,128)(2,1)} fusion(f32[64,3,3584]{2,1,0:T(4,128)} %reshape.91, f32[64,3]{1,0:T(8,128)S(1)} %mul.56, pred[64,3]{1,0:T(8,128)(4,1)S(1)} %lt.27), kind=kLoop, calls=%fused_computation.14 | loop fusion | flops 2064384 | bytes 4129728 | tf_op jit(solution)/shard_map/convert_element_type | solution.py:80
  27.7 13.6 %all-to-all-start.2 = ((bf16[64,3,3584]{2,1,0:T(4,128)(2,1)}), bf16[64,3,3584]{2,1,0:T(4,128)(2,1)}, u32[]{:S(2)}, u32[]{:S(2)}) async-start(bf16[64,3,3584]{2,1,0:T(4,128)(2,1)} %select_convert_fusion), calls=%async_computation.2 | async-start | bytes 3670016 | tf_op jit(solution)/shard_map/all_to_all | solution.py:81
  41.3 0.0 copy-done
  41.3 2.5 gather_fusion
  43.8 3.9 %gather.18 = bf16[64,3,3584]{2,1,0:T(4,128)(2,1)} reshape(bf16[192,3584]{1,0:T(8,128)(2,1)} %gather_fusion) | data formatting | bytes 2752512 | tf_op jit(solution)/shard_map/gather | solution.py:44
  47.7 3.7 %broadcast_select_fusion = bf16[64,3,3584]{2,1,0:T(4,128)(2,1)} fusion(bf16[64,3,3584]{2,1,0:T(4,128)(2,1)} %gather.18, pred[64,3]{1,0:T(8,128)(4,1)S(1)} %lt.27), kind=kLoop, calls=%fused_computation.22 | loop fusion | flops 688128 | bytes 2752704 | tf_op jit(solution)/shard_map/jit(_where)/select_n | solution.py:44
  51.3 34.2 %all-to-all-done.2 = bf16[64,3,3584]{2,1,0:T(4,128)(2,1)} async-done(((bf16[64,3,3584]{2,1,0:T(4,128)(2,1)}), bf16[64,3,3584]{2,1,0:T(4,128)(2,1)}, u32[]{:S(2)}, u32[]{:S(2)}) %all-to-all-start.2) | async-done | bytes 1376288 | tf_op jit(solution)/shard_map/all_to_all | solution.py:81
  85.5 7.0 %all-to-all-start = ((bf16[64,3,3584]{2,1,0:T(4,128)(2,1)}), bf16[64,3,3584]{2,1,0:T(4,128)(2,1)}, u32[]{:S(2)}, u32[]{:S(2)}) async-start(bf16[64,3,3584]{2,1,0:T(4,128)(2,1)} %broadcast_select_fusion), calls=%async_computation | async-start | bytes 3670016 | tf_op jit(solution)/shard_map/all_to_all | solution.py:45
  92.5 0.2 reduce-scatter.3.cloned.1.call-start
  92.7 4.1 %reshape.85 = bf16[192,3584]{1,0:T(8,128)(2,1)} reshape(bf16[64,3,3584]{2,1,0:T(4,128)(2,1)} %all-to-all-done.2) | data formatting | bytes 2752512 | tf_op jit(solution)/shard_map/reshape | solution.py:88
  96.8 39.9 %all-to-all-done = bf16[64,3,3584]{2,1,0:T(4,128)(2,1)} async-done(((bf16[64,3,3584]{2,1,0:T(4,128)(2,1)}), bf16[64,3,3584]{2,1,0:T(4,128)(2,1)}, u32[]{:S(2)}, u32[]{:S(2)}) %all-to-all-start) | async-done | bytes 1376288 | tf_op jit(solution)/shard_map/all_to_all | solution.py:45
  136.7 3.0 reshape.80
  139.7 0.0 all-gather.5.cloned.1.call-done
  139.7 6.5 %multiply_convert_fusion.1 = (bf16[192,1024]{1,0:T(8,128)(2,1)S(1)}, f32[192,1024]{1,0:T(8,128)}) fusion(bf16[192,3584]{1,0:T(8,128)(2,1)S(1)} %reshape.80, bf16[1,3584,1024]{1,2,0:T(8,128)(2,1)} %all-gather.5.cloned.1.call-done), kind=kOutput, calls=%fused_computation.25 | convolution fusion | flops 1410269184 | bytes 9895936 | tf_op jit(solution)/shard_map/dot_general | solution.py:60
  146.2 25.6 %all-gather.7.cloned.1.call-done = bf16[1,1024,3584]{2,1,0:T(8,128)(2,1)} async-done(((bf16[1,256,3584]{2,1,0:T(8,128)(2,1)}), bf16[1,1024,3584]{2,1,0:T(8,128)(2,1)}) %all-gather.7.cloned.1.call-update) | async-done | bytes 7340048 | tf_op jit(solution)/shard_map/all_gather | solution.py:58
  171.8 6.2 %fusion.11 = bf16[192,1024]{1,0:T(8,128)(2,1)S(1)} fusion(bf16[192,3584]{1,0:T(8,128)(2,1)} %reshape.85, bf16[1,1024,3584]{2,1,0:T(8,128)(2,1)} %all-gather.7.cloned.1.call-done, f32[192,1024]{1,0:T(8,128)} %get-tuple-element.11), kind=kOutput, calls=%fused_computation.24 | convolution fusion | flops 1411055616 | bytes 9895936 | tf_op jit(solution)/shard_map/dot_general | solution.py:89
  177.9 5.1 %convolution_convert_fusion.1 = bf16[3584,1024]{1,0:T(8,128)(2,1)} fusion(bf16[192,3584]{1,0:T(8,128)(2,1)S(1)} %reshape.80, bf16[192,1024]{1,0:T(8,128)(2,1)S(1)} %fusion.11), kind=kOutput, calls=%fused_computation.7 | convolution fusion | flops 1412956160 | bytes 9109504 | tf_op jit(solution)/shard_map/dot_general | solution.py:101
  183.0 0.0 copy-start.4
  183.0 0.0 reduce-scatter.3.cloned.1.call-update
  183.1 0.0 reduce-scatter.5.cloned.1.call-start
  183.1 1.3 copy-done.4
  184.4 5.2 %convolution_convert_fusion = bf16[1024,3584]{1,0:T(8,128)(2,1)} fusion(bf16[192,1024]{1,0:T(8,128)(2,1)S(1)} %get-tuple-element.10, bf16[192,3584]{1,0:T(8,128)(2,1)S(1)} %copy-done.4), kind=kOutput, calls=%fused_computation.6 | convolution fusion | flops 1412956160 | bytes 9109504 | tf_op jit(solution)/shard_map/dot_general | solution.py:94
  189.5 0.0 reduce-scatter.5.cloned.1.call-update
  189.6 4.8 %fusion.7 = bf16[192,3584]{1,0:T(8,128)(2,1)S(1)} fusion(bf16[3584,4,256]{0,2,1:T(8,128)(2,1)} %bitcast.47, bf16[24,4,8,256]{3,2,1,0:T(8,128)(2,1)S(1)} %bitcast.45), kind=kOutput, calls=%fused_computation.21 | convolution fusion | flops 1414103040 | bytes 9109504 | tf_op jit(solution)/shard_map/rkf,dkf->krd/dot_general | solution.py:107
  194.4 2.2 reshape.88
  196.6 10.9 %all-to-all-start.3 = ((bf16[64,3,3584]{2,1,0:T(4,128)(2,1)}), bf16[64,3,3584]{2,1,0:T(4,128)(2,1)}, u32[]{:S(2)}, u32[]{:S(2)}) async-start(bf16[64,3,3584]{2,1,0:T(4,128)(2,1)} %reshape.88), calls=%async_computation.3 | async-start | bytes 3670016 | tf_op jit(solution)/shard_map/all_to_all | solution.py:111
  207.4 4.9 %fusion.6 = bf16[192,3584]{1,0:T(8,128)(2,1)S(1)} fusion(bf16[4,256,3584]{2,1,0:T(8,128)(2,1)} %bitcast.46, bf16[24,4,8,256]{3,2,1,0:T(8,128)(2,1)S(1)} %bitcast.44), kind=kOutput, calls=%fused_computation.20 | convolution fusion | flops 1414103040 | bytes 9109504 | tf_op jit(solution)/shard_map/rkf,kfd->krd/dot_general | solution.py:64
  212.4 2.1 reshape.83
  214.5 37.2 %all-to-all-done.3 = bf16[64,3,3584]{2,1,0:T(4,128)(2,1)} async-done(((bf16[64,3,3584]{2,1,0:T(4,128)(2,1)}), bf16[64,3,3584]{2,1,0:T(4,128)(2,1)}, u32[]{:S(2)}, u32[]{:S(2)}) %all-to-all-start.3) | async-done | bytes 1376288 | tf_op jit(solution)/shard_map/all_to_all | solution.py:111
  251.7 7.0 %all-to-all-start.1 = ((bf16[64,3,3584]{2,1,0:T(4,128)(2,1)}), bf16[64,3,3584]{2,1,0:T(4,128)(2,1)}, u32[]{:S(2)}, u32[]{:S(2)}) async-start(bf16[64,3,3584]{2,1,0:T(4,128)(2,1)} %reshape.83), calls=%async_computation.1 | async-start | bytes 3670016 | tf_op jit(solution)/shard_map/all_to_all | solution.py:68
  258.7 3.0 reshape.89
  261.7 1.2 concatenate.7
  262.9 40.2 %all-to-all-done.1 = bf16[64,3,3584]{2,1,0:T(4,128)(2,1)} async-done(((bf16[64,3,3584]{2,1,0:T(4,128)(2,1)}), bf16[64,3,3584]{2,1,0:T(4,128)(2,1)}, u32[]{:S(2)}, u32[]{:S(2)}) %all-to-all-start.1) | async-done | bytes 1376288 | tf_op jit(solution)/shard_map/all_to_all | solution.py:68
  303.1 3.0 reshape.84
  306.0 1.2 concatenate.6
  307.2 5.5 %gather_fusion.4 = bf16[192,3584]{1,0:T(8,128)(2,1)} fusion(bf16[193,3584]{1,0:T(8,128)(2,1)} %concatenate.7, s32[1024]{0:T(1024)S(1)} %pad_clamp_fusion), kind=kCustom, calls=%fused_computation.4 | custom fusion | bytes 2753280 | tf_op jit(solution)/shard_map/gather | solution.py:33
  312.7 0.0 copy-start.1
  312.7 5.5 %gather_fusion.1 = bf16[192,3584]{1,0:T(8,128)(2,1)} fusion(bf16[193,3584]{1,0:T(8,128)(2,1)} %concatenate.6, s32[1024]{0:T(1024)S(1)} %pad_clamp_fusion), kind=kCustom, calls=%fused_computation.1 | custom fusion | bytes 2753280 | tf_op jit(solution)/shard_map/gather | solution.py:33
  318.2 4.8 %fusion.5 = (f32[192]{0:T(256)}, bf16[192,3584]{1,0:T(8,128)(2,1)}, bf16[192,3584]{1,0:T(8,128)(2,1)}) fusion(bf16[192,3584]{1,0:T(8,128)(2,1)} %gather_fusion.1, bf16[192,3584]{1,0:T(8,128)(2,1)S(1)} %copy-done.3, f32[192]{0:T(256)S(1)} %copy-done.2, bf16[192,3584]{1,0:T(8,128)(2,1)} %gather_fusion.4), kind=kLoop, calls=%fused_computation.18 | loop fusion | flops 6192960 | bytes 6882816 | tf_op jit(solution)/shard_map/reduce_sum | solution.py:78
  323.1 0.0 reduce-scatter.3.cloned.1.call-done
  323.1 14.0 %reduce-scatter.5.cloned.1.call-done = bf16[256,3584]{1,0:T(8,128)(2,1)} async-done(((bf16[1024,3584]{1,0:T(8,128)(2,1)}), bf16[256,3584]{1,0:T(8,128)(2,1)}) %reduce-scatter.5.cloned.1.call-update) | async-done | bytes 1835024 | tf_op jit(solution)/shard_map/reduce_scatter | solution.py:93
  337.1 0.0 copy-done.1
  (10 shorter events, 0.1 us)
Async XLA Ops:
  7.2 34.1 %copy-start = (bf16[192,3584]{1,0:T(8,128)(2,1)S(1)}, bf16[192,3584]{1,0:T(8,128)(2,1)}, u32[]{:S(2)}) copy-start(bf16[192,3584]{1,0:T(8,128)(2,1)} %param.6) | copy-start | bytes 4128772
  7.2 132.5 %all-gather.5.cloned.1.call-start = ((), (), s32[]{:S(2)}) async-start(), calls=%async_computation.8 | async-start | bytes 9175040 | tf_op jit(solution)/shard_map/all_gather | solution.py:57
  11.1 0.8 copy-start.5
  11.1 3.1 copy-start.3
  11.2 160.6 %all-gather.7.cloned.1.call-start = ((), (), s32[]{:S(2)}) async-start(), calls=%async_computation.9 | async-start | bytes 9175040 | tf_op jit(solution)/shard_map/all_gather | solution.py:58
  16.7 4.5 %copy-start.2 = (f32[192]{0:T(256)S(1)}, f32[192]{0:T(256)}, u32[]{:S(2)}) copy-start(f32[192]{0:T(256)} %param.8) | copy-start | bytes 2308
  27.7 57.8 %all-to-all-start.2 = ((bf16[64,3,3584]{2,1,0:T(4,128)(2,1)}), bf16[64,3,3584]{2,1,0:T(4,128)(2,1)}, u32[]{:S(2)}, u32[]{:S(2)}) async-start(bf16[64,3,3584]{2,1,0:T(4,128)(2,1)} %select_convert_fusion), calls=%async_computation.2 | async-start | bytes 3670016 | tf_op jit(solution)/shard_map/all_to_all | solution.py:81
  85.5 51.2 %all-to-all-start = ((bf16[64,3,3584]{2,1,0:T(4,128)(2,1)}), bf16[64,3,3584]{2,1,0:T(4,128)(2,1)}, u32[]{:S(2)}, u32[]{:S(2)}) async-start(bf16[64,3,3584]{2,1,0:T(4,128)(2,1)} %broadcast_select_fusion), calls=%async_computation | async-start | bytes 3670016 | tf_op jit(solution)/shard_map/all_to_all | solution.py:45
  92.5 230.6 %reduce-scatter.3.cloned.1.call-start = ((), (), s32[]{:S(2)}) async-start(), calls=%async_computation.6 | async-start | bytes 9175040 | tf_op jit(solution)/shard_map/reduce_scatter | solution.py:102
  183.0 1.3 copy-start.4
  183.1 154.0 %reduce-scatter.5.cloned.1.call-start = ((), (), s32[]{:S(2)}) async-start(), calls=%async_computation.7 | async-start | bytes 9175040 | tf_op jit(solution)/shard_map/reduce_scatter | solution.py:93
  196.6 55.1 %all-to-all-start.3 = ((bf16[64,3,3584]{2,1,0:T(4,128)(2,1)}), bf16[64,3,3584]{2,1,0:T(4,128)(2,1)}, u32[]{:S(2)}, u32[]{:S(2)}) async-start(bf16[64,3,3584]{2,1,0:T(4,128)(2,1)} %reshape.88), calls=%async_computation.3 | async-start | bytes 3670016 | tf_op jit(solution)/shard_map/all_to_all | solution.py:111
  251.7 51.4 %all-to-all-start.1 = ((bf16[64,3,3584]{2,1,0:T(4,128)(2,1)}), bf16[64,3,3584]{2,1,0:T(4,128)(2,1)}, u32[]{:S(2)}, u32[]{:S(2)}) async-start(bf16[64,3,3584]{2,1,0:T(4,128)(2,1)} %reshape.83), calls=%async_computation.1 | async-start | bytes 3670016 | tf_op jit(solution)/shard_map/all_to_all | solution.py:68
  312.7 24.4 %copy-start.1 = (bf16[192,3584]{1,0:T(8,128)(2,1)S(1)}, bf16[192,3584]{1,0:T(8,128)(2,1)}, u32[]{:S(2)}) copy-start(bf16[192,3584]{1,0:T(8,128)(2,1)} %param.6) | copy-start | bytes 4128772
Sparse Core Ops, SparseCore 0:
  11.3 80.7 all-gather.4
  93.9 77.7 all-gather.6
  183.2 76.0 reduce-scatter.2
  262.2 74.8 reduce-scatter.4
where the time goes:
time: 345 us; the launch traced here: 344 us
  waiting for transfers between devices  192 us (56%)
  local copies, waits for them, and re-layouts  52.6 us (15%)
  starting transfers between devices  38.8 us (11%)
  matrix products  32.6 us (9%)
  between operations  14 us (4%)
  other arithmetic  13.9 us (4%)
    all_to_all x1, waiting for transfers between devices, body(): lax.all_to_all(expert_out.reshape(experts, CAP, model_width), 'expert', s...  40.2 us
    all_to_all x1, waiting for transfers between devices, body(): lax.all_to_all(send_tokens.reshape(experts, CAP, model_width), 'expert',...  39.9 us
    all_to_all x1, waiting for transfers between devices, body(): lax.all_to_all(row_grads.reshape(experts, CAP, model_width), 'expert', sp...  37.2 us
    all_to_all x1, waiting for transfers between devices, body(): lax.all_to_all(send_grads.reshape(experts, CAP, model_width), 'expert', s...  34.2 us
    all_gather x1, waiting for transfers between devices, body(): lax.all_gather(down_local, 'replica', axis=0, tiled=True)  25.6 us
    reduce_scatter x1, waiting for transfers between devices, body(): lax.psum_scatter(lax.dot_general(hidden, out_grad, contract_first, prefer...  14 us
    all_to_all x1, starting transfers between devices, body(): lax.all_to_all(send_grads.reshape(experts, CAP, model_width), 'expert', s...  13.6 us
    gather x2, local copies, waits for them, and re-layouts, to_tokens(): return padded[slot_of]  11 us
  transfers between devices with their start and end apart: 8, of which 6 were waited for; matrix products, arithmetic and copies ran while one was open for 24% of the time, Pallas kernels for 0%

commit v1 on v0

v1 whole, which is shorter than its diff:
```python
import functools
import math

import jax
import jax.numpy as jnp
import numpy as np
from jax import lax
from jax.experimental import pallas as pl
from jax.experimental.pallas import tpu as pltpu
from jax.sharding import PartitionSpec as P

CAP = 3
CHUNK = 512
MESH = pl.DeviceIdType.MESH
F32 = jnp.float32
BF16 = jnp.bfloat16
NN = (((1,), (0,)), ((), ()))
NT = (((1,), (1,)), ((), ()))
TN = (((0,), (0,)), ((), ()))


def mm(a, b, dims=NN):
    return lax.dot_general(a, b, dims, preferred_element_type=F32)


def wait_for(ref, sem):
    pltpu.make_async_copy(ref, ref, sem).wait()


def pack(rows, parts, half):
    m = rows.shape[0] // parts
    return [
        jnp.concatenate(
            [rows[p * m:(p + 1) * m, :half], rows[p * m:(p + 1) * m, half:]], axis=0
        ).astype(BF16)
        for p in range(parts)
    ]


def unpack(blocks, parts):
    m = blocks.shape[1] // 2
    wide = [blocks[p].astype(F32) for p in range(parts)]
    left = jnp.concatenate([b[:m] for b in wide], axis=0)
    right = jnp.concatenate([b[m:] for b in wide], axis=0)
    return jnp.concatenate([left, right], axis=1).astype(BF16)


def kernel(
    side, chunks,
    tok, cot, w_row, route_row, swap, wu, wd,
    mixed, token_grads, combine_grads, dwu, dwd,
    send_a, send_b, recv_a, recv_b, xg, wu_far, wd_far, acc, hid, pg,
    out_send, out_recv, dwu_send, dwd_send, dwu_recv, dwd_recv,
    pick, pick_t, w_col, cg, source,
    a_out, a_in, b_out, b_in, y_out, y_in, f_out, f_in, o_out, o_in, d_out, d_in,
):
    nt, width = tok.shape
    slots = side * side * CAP
    half = CHUNK // 2
    expert, y = lax.axis_index("expert"), lax.axis_index("replica")
    z, k = expert // side, expert % side
    row_pal = (expert, y + 1 - 2 * (y % 2))
    block_pal = (expert, 3 - y)
    steps = 2 * chunks

    barrier = pltpu.get_barrier_semaphore()
    for d in range(1, side):
        pl.semaphore_signal(barrier, inc=1, device_id=((z + d) % side * side + k, y), device_id_type=MESH)
        pl.semaphore_signal(barrier, inc=1, device_id=(z * side + (k + d) % side, y), device_id_type=MESH)
    pl.semaphore_signal(barrier, inc=1, device_id=row_pal, device_id_type=MESH)
    pl.semaphore_signal(barrier, inc=1, device_id=block_pal, device_id_type=MESH)

    down = lax.broadcasted_iota(jnp.int32, (nt, nt), 0)
    across = lax.broadcasted_iota(jnp.int32, (nt, nt), 1)
    eye = down == across
    routes = jnp.broadcast_to(route_row[...].astype(F32), (nt, nt))
    route_col = jnp.sum(jnp.where(eye, routes, 0.0), axis=1, keepdims=True)
    w_col[...] = jnp.sum(jnp.where(eye, jnp.broadcast_to(w_row[...], (nt, nt)), 0.0), axis=1, keepdims=True)
    same = routes == route_col
    rank_row = jnp.sum(jnp.where(same & (down < across), 1.0, 0.0), axis=0, keepdims=True)
    rank_col = jnp.sum(jnp.where(same & (across < down), 1.0, 0.0), axis=1, keepdims=True)
    limit = float(side * side)
    slot_row = jnp.where(routes[:1] < limit, routes[:1] * CAP + rank_row, float(slots))
    slot_col = jnp.where(route_col < limit, route_col * CAP + rank_col, float(slots))
    at_slot = lax.broadcasted_iota(jnp.int32, (slots, nt), 0).astype(F32)
    pick[...] = jnp.where(at_slot == slot_row, 1.0, 0.0).astype(BF16)
    at_slot = lax.broadcasted_iota(jnp.int32, (nt, slots), 1).astype(F32)
    pick_t[...] = jnp.where(at_slot == slot_col, 1.0, 0.0).astype(BF16)
    acc[...] = jnp.zeros_like(acc)
    cg[...] = jnp.zeros_like(cg)

    pl.semaphore_wait(barrier, 2 * side)

    def columns(j):
        return pl.ds(pl.multiple_of(j * CHUNK, CHUNK), CHUNK)

    order = sorted(range(1, side), key=lambda d: -min(d, side - d))

    def exchange_a(i, j):
        for d in order:
            to = (z + d) % side
            pltpu.make_async_remote_copy(
                send_a.at[j, to], recv_a.at[i, z], a_out.at[j], a_in.at[i],
                device_id=(to * side + k, y), device_id_type=MESH,
            ).start()
        pltpu.make_async_copy(send_a.at[j, z], recv_a.at[i, z], a_in.at[i]).start()

    def exchange_b(i, j):
        for d in order:
            to = (k + d) % side
            pltpu.make_async_remote_copy(
                send_b.at[j, to], recv_b.at[i, k], b_out.at[j], b_in.at[i],
                device_id=(z * side + to, y), device_id_type=MESH,
            ).start()
        pltpu.make_async_copy(send_b.at[j, k], recv_b.at[i, k], b_in.at[i]).start()

    def sent_a(j):
        wait_for(send_a.at[j, pl.ds(0, side - 1)], a_out.at[j])

    def sent_b(j):
        wait_for(send_b.at[j, pl.ds(0, side - 1)], b_out.at[j])

    def swapped(ref, i):
        blocks = ref[i]
        flat = blocks.reshape(blocks.shape[0] * blocks.shape[1], half)
        return mm(swap[...], flat).astype(BF16).reshape(blocks.shape)

    def far_weight(i, go):
        j = i % chunks

        @pl.when(i < chunks)
        def _():
            copy = pltpu.make_async_remote_copy(
                wu.at[columns(j), :], wu_far.at[j], f_out.at[i], f_in.at[i],
                device_id=block_pal, device_id_type=MESH)
            go(copy)

        @pl.when(i >= chunks)
        def _():
            copy = pltpu.make_async_remote_copy(
                wd.at[:, columns(j)], wd_far.at[j], f_out.at[i], f_in.at[i],
                device_id=block_pal, device_id_type=MESH)
            go(copy)

    def step_a(i):
        j = i % chunks

        @pl.when(i < chunks)
        def _():
            source[...] = tok[:, columns(j)]

        @pl.when(i >= chunks)
        def _():
            sent_a(j)
            source[...] = (w_col[...] * cot[:, columns(j)].astype(F32)).astype(BF16)

        for p, block in enumerate(pack(mm(pick[...], source[...]), side, half)):
            send_a[j, p] = block
        exchange_a(i, j)

    def step_b(i):
        j = i % chunks
        wait_for(recv_a.at[i], a_in.at[i])

        @pl.when(i >= chunks)
        def _():
            sent_b(j)

        send_b[j] = swapped(recv_a, i)
        exchange_b(i, j)

    def row_copy(i):
        return pltpu.make_async_remote_copy(
            xg.at[i, pl.ds(0, slots)], xg.at[i, pl.ds(slots, slots)], y_out.at[i], y_in.at[i],
            device_id=row_pal, device_id_type=MESH)

    def step_c(i):
        wait_for(recv_b.at[i], b_in.at[i])
        xg[i, pl.ds(0, slots)] = unpack(recv_b[i], side)
        row_copy(i).start()

    def step_d(i):
        j = i % chunks
        row_copy(i).wait_recv()
        far_weight(i, lambda copy: copy.wait_recv())

        @pl.when(i < chunks)
        def _():
            acc[0] += mm(xg[i], wu[columns(j), :])
            acc[1] += mm(xg[i], wu_far[j])

        @pl.when(i >= chunks)
        def _():
            acc[2] += mm(xg[i], wd[:, columns(j)], NT)
            acc[3] += mm(xg[i], wd_far[j], NT)

    def at(i, lag, step):
        @pl.when((i >= lag) & (i < steps + lag))
        def _():
            step(i - lag)

    AHEAD = 3
    for i in range(AHEAD):
        far_weight(jnp.int32(i), lambda copy: copy.start())

    LAG_D = 4

    def gather(i, _):
        at(i, 0, step_a)

        @pl.when(i + AHEAD < steps)
        def _():
            far_weight(i + AHEAD, lambda copy: copy.start())

        at(i, 1, step_b)
        at(i, 2, step_c)
        at(i, LAG_D, step_d)
        return 0

    lax.fori_loop(0, steps + LAG_D, gather, 0)

    for b in range(2):
        pre = acc[b]
        s = 1.0 / (1.0 + jnp.exp(-pre))
        hid[b] = (pre * s).astype(BF16)
        pg[b] = (acc[2 + b] * (s * (1.0 + pre * (1.0 - s)))).astype(BF16)


    def out_copy(i):
        j = i % chunks
        return pltpu.make_async_remote_copy(
            out_send.at[j], out_recv.at[i], o_out.at[j], o_in.at[i],
            device_id=row_pal, device_id_type=MESH)

    def dwd_copy(i):
        j = i % chunks
        return pltpu.make_async_remote_copy(
            dwd_send.at[j], dwd_recv.at[j], d_out.at[i], d_in.at[i],
            device_id=block_pal, device_id_type=MESH)

    def dwu_copy(i):
        j = i % chunks
        return pltpu.make_async_remote_copy(
            dwu_send.at[j], dwu_recv.at[j], d_out.at[i], d_in.at[i],
            device_id=block_pal, device_id_type=MESH)

    def out_rows(j, rows):
        return mm(hid[0, rows], wd[:, columns(j)]) + mm(hid[1, rows], wd_far[j])

    def grad_rows(j, rows):
        return mm(pg[0, rows], wu[columns(j), :], NT) + mm(pg[1, rows], wu_far[j], NT)

    near, far = pl.ds(0, slots), pl.ds(slots, slots)

    def step_e(i):
        j = i % chunks

        @pl.when(i < chunks)
        def _():
            out_send[j] = out_rows(j, far).astype(BF16)
            out_copy(i).start()
            dwd_send[j] = mm(hid[1], xg[chunks + j], TN).astype(BF16)
            dwd_copy(i).start()

        @pl.when(i >= chunks)
        def _():
            out_copy(i).wait_send()
            out_send[j] = grad_rows(j, far).astype(BF16)
            out_copy(i).start()
            dwu_send[j] = mm(xg[j], pg[1], TN).astype(BF16)
            dwu_copy(i).start()

    def step_f(i):
        j = i % chunks
        out_copy(i).wait_recv()
        sent_b(j)

        @pl.when(i < chunks)
        def _():
            for p, block in enumerate(pack(out_rows(j, near) + out_recv[i].astype(F32), side, half)):
                send_b[j, p] = block

        @pl.when(i >= chunks)
        def _():
            for p, block in enumerate(pack(grad_rows(j, near) + out_recv[i].astype(F32), side, half)):
                send_b[j, p] = block

        exchange_b(steps + i, j)

    def step_g(i):
        j = i % chunks
        wait_for(recv_b.at[steps + i], b_in.at[steps + i])
        sent_a(j)
        send_a[j] = swapped(recv_b, steps + i)
        exchange_a(steps + i, j)

    def step_h(i):
        j = i % chunks
        wait_for(recv_a.at[steps + i], a_in.at[steps + i])
        rows = mm(pick_t[...], unpack(recv_a[steps + i], side))
        scaled = (w_col[...] * rows).astype(BF16)

        @pl.when(i < chunks)
        def _():
            mixed[:, columns(j)] = scaled
            cg[...] += jnp.sum(rows * cot[:, columns(j)].astype(F32), axis=1, keepdims=True)

        @pl.when(i >= chunks)
        def _():
            token_grads[:, columns(j)] = scaled

    def step_i(i):
        j = i % chunks

        @pl.when(i < chunks)
        def _():
            dwd_copy(i).wait_recv()
            dwd[:, columns(j)] = (mm(hid[0], xg[chunks + j], TN) + dwd_recv[j].astype(F32)).astype(BF16)

        @pl.when(i >= chunks)
        def _():
            dwu_copy(i).wait_recv()
            dwu[columns(j), :] = (mm(xg[j], pg[0], TN) + dwu_recv[j].astype(F32)).astype(BF16)

    LAG_I = 4

    def scatter(i, _):
        at(i, 0, step_e)
        at(i, 1, step_f)
        at(i, 2, step_g)
        at(i, 3, step_h)
        at(i, LAG_I, step_i)
        return 0

    lax.fori_loop(0, steps + LAG_I, scatter, 0)

    combine_grads[...] = jnp.sum(jnp.where(eye, jnp.broadcast_to(cg[...], (nt, nt)), 0.0), axis=0, keepdims=True)

    def drain(j, _):
        sent_a(j)
        sent_b(j)
        out_copy(j + chunks).wait_send()
        dwd_copy(j).wait_send()
        dwu_copy(j + chunks).wait_send()
        return 0

    lax.fori_loop(0, chunks, drain, 0)

    def drain_all(i, _):
        row_copy(i).wait_send()
        far_weight(i, lambda copy: copy.wait_send())
        return 0

    lax.fori_loop(0, steps, drain_all, 0)


def swap_matrix(side):
    n = side * 2 * side * CAP
    index = np.arange(n).reshape(side, 2, side, CAP)
    source = index.transpose(2, 1, 0, 3).reshape(-1)
    matrix = np.zeros((n, n), np.float32)
    matrix[np.arange(n), source] = 1.0
    return matrix.astype(jnp.bfloat16)


def body(side, tokens, routes, combine_weights, up_weight, down_weight, cotangent):
    nt, width = tokens.shape
    block = up_weight.shape[2]
    chunks = width // CHUNK
    slots = side * side * CAP
    half = CHUNK // 2
    steps = 2 * chunks
    vmem = pl.BlockSpec(memory_space=pltpu.VMEM)
    message = (side, 2 * side * CAP, half)
    dma = pltpu.SemaphoreType.DMA
    mixed, token_grads, combine_grads, up_grads, down_grads = pl.pallas_call(
        functools.partial(kernel, side, chunks),
        out_shape=(
            jax.ShapeDtypeStruct((nt, width), BF16),
            jax.ShapeDtypeStruct((nt, width), BF16),
            jax.ShapeDtypeStruct((1, nt), F32),
            jax.ShapeDtypeStruct((width, block), BF16),
            jax.ShapeDtypeStruct((block, width), BF16),
        ),
        in_specs=[vmem] * 7,
        out_specs=(vmem,) * 5,
        scratch_shapes=[
            pltpu.VMEM((chunks,) + message, BF16),
            pltpu.VMEM((chunks,) + message, BF16),
            pltpu.VMEM((2 * steps,) + message, BF16),
            pltpu.VMEM((2 * steps,) + message, BF16),
            pltpu.VMEM((steps, 2 * slots, CHUNK), BF16),
            pltpu.VMEM((chunks, CHUNK, block), BF16),
            pltpu.VMEM((chunks, block, CHUNK), BF16),
            pltpu.VMEM((4, 2 * slots, block), F32),
            pltpu.VMEM((2, 2 * slots, block), BF16),
            pltpu.VMEM((2, 2 * slots, block), BF16),
            pltpu.VMEM((chunks, slots, CHUNK), BF16),
            pltpu.VMEM((steps, slots, CHUNK), BF16),
            pltpu.VMEM((chunks, CHUNK, block), BF16),
            pltpu.VMEM((chunks, block, CHUNK), BF16),
            pltpu.VMEM((chunks, CHUNK, block), BF16),
            pltpu.VMEM((chunks, block, CHUNK), BF16),
            pltpu.VMEM((slots, nt), BF16),
            pltpu.VMEM((nt, slots), BF16),
            pltpu.VMEM((nt, 1), F32),
            pltpu.VMEM((nt, 1), F32),
            pltpu.VMEM((nt, CHUNK), BF16),
            dma((chunks,)), dma((2 * steps,)),
            dma((chunks,)), dma((2 * steps,)),
            dma((steps,)), dma((steps,)),
            dma((steps,)), dma((steps,)),
            dma((chunks,)), dma((steps,)),
            dma((steps,)), dma((steps,)),
        ],
        compiler_params=pltpu.CompilerParams(
            collective_id=0, has_side_effects=True, vmem_limit_bytes=60 * 1024 * 1024
        ),
    )(
        tokens, cotangent, combine_weights[None], routes[None],
        jnp.asarray(swap_matrix(side)), up_weight[0], down_weight[0],
    )
    return mixed, token_grads, combine_grads[0], up_grads[None], down_grads[None]


def solution(mesh):
    side = math.isqrt(mesh.shape["expert"])
    row, vector = P(("expert", "replica"), None), P(("expert", "replica"))
    up, down = P("expert", None, "replica"), P("expert", "replica", None)
    return jax.shard_map(
        functools.partial(body, side),
        mesh=mesh,
        in_specs=(row, vector, vector, up, down, row),
        out_specs=(row, row, vector, up, down),
        check_vma=False,
    )
```

time: 345 us -> 188 us (0.54)
  waiting for transfers between devices: 192 us -> 0 us
  Pallas kernels: 0 us -> 180 us
  local copies, waits for them, and re-layouts: 52.6 us -> 8 us
  starting transfers between devices: 38.8 us -> 0 us
  matrix products: 32.6 us -> 0 us
  other arithmetic: 13.9 us -> 0 us
  between operations: 14 us -> 0.65 us
    pallas_call x0 -> x1, Pallas kernels: none -> 180 us  [body(): pl.pallas_call(functools.partial(kernel, side, chunks), out_shape=(jax.Sh...]
    all_to_all x4 -> x0, waiting for transfers between devices: 151 us -> none  [the longest x1 40.2 us: body(): lax.all_to_all(expert_out.reshape(experts, CAP, model_width), 'expert', s...]
    all_to_all x4 -> x0, starting transfers between devices: 38.4 us -> none  [the longest x1 13.6 us: body(): lax.all_to_all(send_grads.reshape(experts, CAP, model_width), 'expert', s...]
    dot_general x6 -> x0, matrix products: 32.6 us -> none  [the longest x1 6.49 us: body(): pre_act = jnp.dot(arrived, up_full, preferred_element_type=jnp.float32)]
    all_gather x2 -> x0, waiting for transfers between devices: 25.6 us -> none  [the longest x1 25.6 us: body(): lax.all_gather(down_local, 'replica', axis=0, tiled=True)]
    gather x6 -> x0, local copies, waits for them, and re-layouts: 21.5 us -> none  [the longest x2 11 us: to_tokens(): return padded[slot_of]]
    reshape x6 -> x0, local copies, waits for them, and re-layouts: 17.4 us -> none  [the longest x2 5.95 us: to_tokens(): flat_rows = returned.reshape(-1, model_width)]
    reduce_scatter x2 -> x0, waiting for transfers between devices: 14 us -> none  [the longest x1 14 us: body(): lax.psum_scatter(lax.dot_general(hidden, out_grad, contract_first, prefer...]
  transfers between devices with their start and end apart: 8 -> 0, of which waited for: 6 -> 0; matrix products, arithmetic and copies ran while one was open for 24% -> 0% of each run, Pallas kernels for 0% -> 0%
where the time goes in v1:
time: 188 us
  Pallas kernels  180 us (96%)
  local copies, waits for them, and re-layouts  8 us (4%)
    pallas_call x1, Pallas kernels, body(): pl.pallas_call(functools.partial(kernel, side, chunks), out_shape=(jax.Sh...  180 us
    unnamed x13, local copies, waits for them, and re-layouts  8 us

profile of v1, /device:TPU:1, one launch (start us, length us, event | category | flops | bytes accessed | tf_op | source)
XLA Modules:
  0.0 188.3 jit_solution(1559335665389384322)
XLA Ops:
  0.6 179.6 %shard_map.110 = (bf16[192,3584]{1,0:T(8,128)(2,1)}, bf16[192,3584]{1,0:T(8,128)(2,1)}, f32[1,192]{1,0:T(1,128)}, bf16[3584,256]{1,0:T(8,128)(2,1)}, bf16[256,3584]{1,0:T(8,128)(2,1)}) custom-call(bf16[192,3584]{1,0:T(8,128)(2,1)} %tok.1, bf16[192,3584]{1,0:T(8,128)(2,1)} %cot.1, f32[1,192]{1,0:T(1,128)} %bitcast.11, s32[1,192]{1,0:T(1,128)} %bitcast.12, ...), custom_call_target="tpu_custom_call" | custom-call | tf_op jit(solution)/shard_map/pallas_call | solution.py:376
  180.3 0.0 copy-start.2
  180.3 2.6 %copy.17 = bf16[192,3584]{1,0:T(8,128)(2,1)} copy(bf16[192,3584]{1,0:T(8,128)(2,1)} %get-tuple-element.20) | data formatting | bytes 2752512
  182.9 0.0 copy-done.2
  182.9 0.0 copy-start.3
  182.9 0.0 copy-start.1
  182.9 1.1 copy.18
  184.0 0.0 copy-done.3
  184.0 0.6 copy.19
  184.5 0.4 copy-done.1
  184.9 0.0 copy-start
  184.9 1.2 copy.20
  186.1 0.9 copy-done
  187.0 1.2 copy.21
Async XLA Ops:
  180.3 2.6 %copy-start.2 = (bf16[192,3584]{1,0:T(8,128)(2,1)S(1)}, bf16[192,3584]{1,0:T(8,128)(2,1)}, u32[]{:S(2)}) copy-start(bf16[192,3584]{1,0:T(8,128)(2,1)} %get-tuple-element.21) | copy-start | bytes 4128772
  182.9 1.1 copy-start.3
  182.9 2.0 %copy-start.1 = (bf16[3584,256]{1,0:T(8,128)(2,1)S(1)}, bf16[3584,256]{1,0:T(8,128)(2,1)}, u32[]{:S(2)}) copy-start(bf16[3584,256]{1,0:T(8,128)(2,1)} %get-tuple-element.13) | copy-start | bytes 5505028
  184.9 2.2 %copy-start = (bf16[256,3584]{1,0:T(8,128)(2,1)S(1)}, bf16[256,3584]{1,0:T(8,128)(2,1)}, u32[]{:S(2)}) copy-start(bf16[256,3584]{1,0:T(8,128)(2,1)} %get-tuple-element.14) | copy-start | bytes 5505028

commit v2 on v1

--- a/solution.py
+++ b/solution.py
@@ -11,6 +11,9 @@
 
 CAP = 3
 CHUNK = 512
+LAG_B, LAG_C, LAG_D = 1, 2, 4
+LAG_F, LAG_G, LAG_H, LAG_W, LAG_I = 2, 3, 5, 4, 8
+AHEAD = 6
 MESH = pl.DeviceIdType.MESH
 F32 = jnp.float32
 BF16 = jnp.bfloat16
@@ -47,20 +50,23 @@
 
 def kernel(
     side, chunks,
-    tok, cot, w_row, route_row, swap, wu, wd,
+    tok_hbm, cot_hbm, w_row, route_row, swap, wu_hbm, wd_hbm,
     mixed, token_grads, combine_grads, dwu, dwd,
+    tok, cot, wu, wd,
     send_a, send_b, recv_a, recv_b, xg, wu_far, wd_far, acc, hid, pg,
     out_send, out_recv, dwu_send, dwd_send, dwu_recv, dwd_recv,
     pick, pick_t, w_col, cg, source,
-    a_out, a_in, b_out, b_in, y_out, y_in, f_out, f_in, o_out, o_in, d_out, d_in,
+    a_out, a_in, b_out, b_in, y_out, y_in, f_out, f_in, o_out, o_in, d_out, d_in, load, load_w,
 ):
     nt, width = tok.shape
     slots = side * side * CAP
     half = CHUNK // 2
     expert, y = lax.axis_index("expert"), lax.axis_index("replica")
     z, k = expert // side, expert % side
-    row_pal = (expert, y + 1 - 2 * (y % 2))
-    block_pal = (expert, 3 - y)
+    core = k % 2
+    odd = 1 - (y + core) % 2 * 2
+    row_pal = (expert, (y + odd + 4) % 4)
+    block_pal = (expert, (y - odd + 4) % 4)
     steps = 2 * chunks
 
     barrier = pltpu.get_barrier_semaphore()
@@ -69,6 +75,45 @@
         pl.semaphore_signal(barrier, inc=1, device_id=(z * side + (k + d) % side, y), device_id_type=MESH)
     pl.semaphore_signal(barrier, inc=1, device_id=row_pal, device_id_type=MESH)
     pl.semaphore_signal(barrier, inc=1, device_id=block_pal, device_id_type=MESH)
+
+    def columns(j):
+        return pl.ds(pl.multiple_of(j * CHUNK, CHUNK), CHUNK)
+
+    def tok_load(j):
+        return pltpu.make_async_copy(tok_hbm.at[:, columns(j)], tok.at[:, columns(j)], load.at[j])
+
+    def cot_load(j):
+        return pltpu.make_async_copy(cot_hbm.at[:, columns(j)], cot.at[:, columns(j)], load.at[chunks + j])
+
+    wu_load = pltpu.make_async_copy(wu_hbm, wu, load_w.at[0])
+    wd_load = pltpu.make_async_copy(wd_hbm, wd, load_w.at[1])
+    for j in range(chunks):
+        tok_load(j).start()
+    wu_load.start()
+    for j in range(chunks):
+        cot_load(j).start()
+    wd_load.start()
+
+    def far_weight(i, go):
+        j = i % chunks
+
+        @pl.when(i < chunks)
+        def _():
+            copy = pltpu.make_async_remote_copy(
+                wu_hbm.at[columns(j), :], wu_far.at[j], f_out.at[i], f_in.at[i],
+                device_id=block_pal, device_id_type=MESH)
+            go(copy)
+
+        @pl.when(i >= chunks)
+        def _():
+            copy = pltpu.make_async_remote_copy(
+                wd_hbm.at[:, columns(j)], wd_far.at[j], f_out.at[i], f_in.at[i],
+                device_id=block_pal, device_id_type=MESH)
+            go(copy)
+
+    pl.semaphore_wait(barrier, 2 * side)
+    for i in range(AHEAD):
+        far_weight(jnp.int32(i), lambda copy: copy.start())
 
     down = lax.broadcasted_iota(jnp.int32, (nt, nt), 0)
     across = lax.broadcasted_iota(jnp.int32, (nt, nt), 1)
@@ -89,11 +134,6 @@
     acc[...] = jnp.zeros_like(acc)
     cg[...] = jnp.zeros_like(cg)
 
-    pl.semaphore_wait(barrier, 2 * side)
-
-    def columns(j):
-        return pl.ds(pl.multiple_of(j * CHUNK, CHUNK), CHUNK)
-
     order = sorted(range(1, side), key=lambda d: -min(d, side - d))
 
     def exchange_a(i, j):
@@ -125,33 +165,18 @@
         flat = blocks.reshape(blocks.shape[0] * blocks.shape[1], half)
         return mm(swap[...], flat).astype(BF16).reshape(blocks.shape)
 
-    def far_weight(i, go):
-        j = i % chunks
-
-        @pl.when(i < chunks)
-        def _():
-            copy = pltpu.make_async_remote_copy(
-                wu.at[columns(j), :], wu_far.at[j], f_out.at[i], f_in.at[i],
-                device_id=block_pal, device_id_type=MESH)
-            go(copy)
-
-        @pl.when(i >= chunks)
-        def _():
-            copy = pltpu.make_async_remote_copy(
-                wd.at[:, columns(j)], wd_far.at[j], f_out.at[i], f_in.at[i],
-                device_id=block_pal, device_id_type=MESH)
-            go(copy)
-
     def step_a(i):
         j = i % chunks
 
         @pl.when(i < chunks)
         def _():
+            tok_load(j).wait()
             source[...] = tok[:, columns(j)]
 
         @pl.when(i >= chunks)
         def _():
             sent_a(j)
+            cot_load(j).wait()
             source[...] = (w_col[...] * cot[:, columns(j)].astype(F32)).astype(BF16)
 
         for p, block in enumerate(pack(mm(pick[...], source[...]), side, half)):
@@ -184,6 +209,14 @@
         row_copy(i).wait_recv()
         far_weight(i, lambda copy: copy.wait_recv())
 
+        @pl.when(i == 0)
+        def _():
+            wu_load.wait()
+
+        @pl.when(i == chunks)
+        def _():
+            wd_load.wait()
+
         @pl.when(i < chunks)
         def _():
             acc[0] += mm(xg[i], wu[columns(j), :])
@@ -199,32 +232,19 @@
         def _():
             step(i - lag)
 
-    AHEAD = 3
-    for i in range(AHEAD):
-        far_weight(jnp.int32(i), lambda copy: copy.start())
-
-    LAG_D = 4
-
-    def gather(i, _):
-        at(i, 0, step_a)
-
-        @pl.when(i + AHEAD < steps)
-        def _():
-            far_weight(i + AHEAD, lambda copy: copy.start())
-
-        at(i, 1, step_b)
-        at(i, 2, step_c)
-        at(i, LAG_D, step_d)
-        return 0
-
-    lax.fori_loop(0, steps + LAG_D, gather, 0)
-
-    for b in range(2):
-        pre = acc[b]
-        s = 1.0 / (1.0 + jnp.exp(-pre))
-        hid[b] = (pre * s).astype(BF16)
-        pg[b] = (acc[2 + b] * (s * (1.0 + pre * (1.0 - s)))).astype(BF16)
-
+    def sigmoid(v):
+        return 1.0 / (1.0 + jnp.exp(-v))
+
+    def forward():
+        for b in range(2):
+            pre = acc[b]
+            hid[b] = (pre * sigmoid(pre)).astype(BF16)
+
+    def backward():
+        for b in range(2):
+            pre = acc[b]
+            s = sigmoid(pre)
+            pg[b] = (acc[2 + b] * (s * (1.0 + pre * (1.0 - s)))).astype(BF16)
 
     def out_copy(i):
         j = i % chunks
@@ -259,14 +279,23 @@
         def _():
             out_send[j] = out_rows(j, far).astype(BF16)
             out_copy(i).start()
-            dwd_send[j] = mm(hid[1], xg[chunks + j], TN).astype(BF16)
-            dwd_copy(i).start()
 
         @pl.when(i >= chunks)
         def _():
             out_copy(i).wait_send()
             out_send[j] = grad_rows(j, far).astype(BF16)
             out_copy(i).start()
+
+    def step_w(i):
+        j = i % chunks
+
+        @pl.when(i < chunks)
+        def _():
+            dwd_send[j] = mm(hid[1], xg[chunks + j], TN).astype(BF16)
+            dwd_copy(i).start()
+
+        @pl.when(i >= chunks)
+        def _():
             dwu_send[j] = mm(xg[j], pg[1], TN).astype(BF16)
             dwu_copy(i).start()
 
@@ -322,17 +351,29 @@
             dwu_copy(i).wait_recv()
             dwu[columns(j), :] = (mm(xg[j], pg[0], TN) + dwu_recv[j].astype(F32)).astype(BF16)
 
-    LAG_I = 4
-
-    def scatter(i, _):
-        at(i, 0, step_e)
-        at(i, 1, step_f)
-        at(i, 2, step_g)
-        at(i, 3, step_h)
-        at(i, LAG_I, step_i)
+    begin = chunks + LAG_D
+
+    def turn(n, _):
+        at(n, 0, step_a)
+
+        @pl.when(n + AHEAD < steps)
+        def _():
+            far_weight(n + AHEAD, lambda copy: copy.start())
+
+        at(n, LAG_B, step_b)
+        at(n, LAG_C, step_c)
+        at(n, LAG_D, step_d)
+        pl.when(n == begin - 1)(forward)
+        pl.when(n == begin + chunks - 1)(backward)
+        at(n, begin, step_e)
+        at(n, begin + LAG_F, step_f)
+        at(n, begin + LAG_W, step_w)
+        at(n, begin + LAG_G, step_g)
+        at(n, begin + LAG_H, step_h)
+        at(n, begin + LAG_I, step_i)
         return 0
 
-    lax.fori_loop(0, steps + LAG_I, scatter, 0)
+    lax.fori_loop(0, begin + steps + max(LAG_H, LAG_I), turn, 0)
 
     combine_grads[...] = jnp.sum(jnp.where(eye, jnp.broadcast_to(cg[...], (nt, nt)), 0.0), axis=0, keepdims=True)
 
@@ -352,6 +393,24 @@
         return 0
 
     lax.fori_loop(0, steps, drain_all, 0)
+
+
+PIECES = 4
+
+
+def hand_over(*refs):
+    given, result, stores = refs[:4], refs[5:9], refs[10]
+    copies = []
+    for a in range(4):
+        rows = given[a].shape[0] // PIECES
+        for p in range(PIECES):
+            at = pl.ds(p * rows, rows)
+            copies.append(pltpu.make_async_copy(given[a].at[at], result[a].at[at], stores.at[a * PIECES + p]))
+    for copy in copies:
+        copy.start()
+    refs[9][...] = refs[4][...].reshape(refs[9].shape)
+    for copy in copies:
+        copy.wait()
 
 
 def swap_matrix(side):
@@ -371,20 +430,25 @@
     half = CHUNK // 2
     steps = 2 * chunks
     vmem = pl.BlockSpec(memory_space=pltpu.VMEM)
+    hbm = pl.BlockSpec(memory_space=pl.ANY)
     message = (side, 2 * side * CAP, half)
     dma = pltpu.SemaphoreType.DMA
     mixed, token_grads, combine_grads, up_grads, down_grads = pl.pallas_call(
         functools.partial(kernel, side, chunks),
         out_shape=(
-            jax.ShapeDtypeStruct((nt, width), BF16),
-            jax.ShapeDtypeStruct((nt, width), BF16),
-            jax.ShapeDtypeStruct((1, nt), F32),
-            jax.ShapeDtypeStruct((width, block), BF16),
-            jax.ShapeDtypeStruct((block, width), BF16),
+            pltpu.VMEM((nt, width), BF16),
+            pltpu.VMEM((nt, width), BF16),
+            pltpu.VMEM((1, nt), F32),
+            pltpu.VMEM((width, block), BF16),
+            pltpu.VMEM((block, width), BF16),
         ),
-        in_specs=[vmem] * 7,
+        in_specs=[hbm, hbm, vmem, vmem, vmem, hbm, hbm],
         out_specs=(vmem,) * 5,
         scratch_shapes=[
+            pltpu.VMEM((nt, width), BF16),
+            pltpu.VMEM((nt, width), BF16),
+            pltpu.VMEM((width, block), BF16),
+            pltpu.VMEM((block, width), BF16),
             pltpu.VMEM((chunks,) + message, BF16),
             pltpu.VMEM((chunks,) + message, BF16),
             pltpu.VMEM((2 * steps,) + message, BF16),
@@ -412,15 +476,25 @@
             dma((steps,)), dma((steps,)),
             dma((chunks,)), dma((steps,)),
             dma((steps,)), dma((steps,)),
+            dma((steps,)), dma((2,)),
         ],
         compiler_params=pltpu.CompilerParams(
-            collective_id=0, has_side_effects=True, vmem_limit_bytes=60 * 1024 * 1024
+            collective_id=0, has_side_effects=True, vmem_limit_bytes=50 * 1024 * 1024
         ),
     )(
         tokens, cotangent, combine_weights[None], routes[None],
         jnp.asarray(swap_matrix(side)), up_weight[0], down_weight[0],
     )
-    return mixed, token_grads, combine_grads[0], up_grads[None], down_grads[None]
+    large = (mixed, token_grads, up_grads, down_grads)
+    mixed, token_grads, up_grads, down_grads, combine_grads = pl.pallas_call(
+        hand_over,
+        out_shape=[jax.ShapeDtypeStruct(a.shape, a.dtype) for a in large] + [jax.ShapeDtypeStruct((nt,), F32)],
+        in_specs=[vmem] * 5,
+        out_specs=[hbm] * 4 + [vmem],
+        scratch_shapes=[dma((4 * PIECES,))],
+        compiler_params=pltpu.CompilerParams(vmem_limit_bytes=4 * 1024 * 1024),
+    )(*large, combine_grads)
+    return mixed, token_grads, combine_grads, up_grads[None], down_grads[None]
 
 
 def solution(mesh):

time: 188 us -> 157 us (0.84)
  Pallas kernels: 180 us -> 156 us
  local copies, waits for them, and re-layouts: 8 us -> 0 us
    pallas_call x1 -> x2, Pallas kernels: 180 us -> 156 us  [the longest x1 152 us: body(): pl.pallas_call(functools.partial(kernel, side, chunks), out_shape=(pltpu....]
    unnamed x13 -> x0, local copies, waits for them, and re-layouts: 8 us -> none
where the time goes in v2:
time: 157 us; the launch traced here: 156 us
  Pallas kernels  156 us (99%)
    pallas_call x1, Pallas kernels, body(): pl.pallas_call(functools.partial(kernel, side, chunks), out_shape=(pltpu....  152 us
    pallas_call x1, Pallas kernels, body(): pl.pallas_call(hand_over, out_shape=[jax.ShapeDtypeStruct(a.shape, a.dtyp...  3.4 us

profile of v2, /device:TPU:1, one launch (start us, length us, event | category | flops | bytes accessed | tf_op | source)
XLA Modules:
  0.0 156.3 jit_solution(2742185057179772548)
XLA Ops:
  0.6 152.3 %shard_map.110 = (bf16[192,3584]{1,0:T(8,128)(2,1)S(1)}, bf16[192,3584]{1,0:T(8,128)(2,1)S(1)}, f32[1,192]{1,0:T(1,128)S(1)}, bf16[3584,256]{1,0:T(8,128)(2,1)S(1)}, bf16[256,3584]{1,0:T(8,128)(2,1)S(1)}) custom-call(bf16[192,3584]{1,0:T(8,128)(2,1)} %tok_hbm.1, bf16[192,3584]{1,0:T(8,128)(2,1)} %cot_hbm.1, f32[1,192]{1,0:T(1,128)} %bitcast.8, ...), custom_call_target="tpu_custom_call" | custom-call | tf_op jit(solution)/shard_map/pallas_call | solution.py:436
  152.9 3.4 %shard_map.111 = (bf16[192,3584]{1,0:T(8,128)(2,1)}, bf16[192,3584]{1,0:T(8,128)(2,1)}, bf16[3584,256]{1,0:T(8,128)(2,1)}, bf16[256,3584]{1,0:T(8,128)(2,1)}, f32[192]{0:T(256)}) custom-call(bf16[192,3584]{1,0:T(8,128)(2,1)S(1)} %get-tuple-element.15.refs_0_, bf16[192,3584]{1,0:T(8,128)(2,1)S(1)} %get-tuple-element.16.refs_1_, ...), custom_call_target="tpu_custom_call" | custom-call | tf_op jit(solution)/shard_map/pallas_call | solution.py:489

commit v3 on v2

--- a/solution.py
+++ b/solution.py
@@ -50,9 +50,9 @@
 
 def kernel(
     side, chunks,
-    tok_hbm, cot_hbm, w_row, route_row, swap, wu_hbm, wd_hbm,
+    tok_hbm, cot_hbm, w_hbm, route_hbm, swap_hbm, wu_hbm, wd_hbm,
     mixed, token_grads, combine_grads, dwu, dwd,
-    tok, cot, wu, wd,
+    tok, cot, wu, wd, w_row, route_row, swap,
     send_a, send_b, recv_a, recv_b, xg, wu_far, wd_far, acc, hid, pg,
     out_send, out_recv, dwu_send, dwd_send, dwu_recv, dwd_recv,
     pick, pick_t, w_col, cg, source,
@@ -87,6 +87,12 @@
 
     wu_load = pltpu.make_async_copy(wu_hbm, wu, load_w.at[0])
     wd_load = pltpu.make_async_copy(wd_hbm, wd, load_w.at[1])
+    small = [
+        pltpu.make_async_copy(a, b, load_w.at[2 + i])
+        for i, (a, b) in enumerate(((w_hbm, w_row), (route_hbm, route_row), (swap_hbm, swap)))
+    ]
+    for copy in small:
+        copy.start()
     for j in range(chunks):
         tok_load(j).start()
     wu_load.start()
@@ -114,6 +120,9 @@
     pl.semaphore_wait(barrier, 2 * side)
     for i in range(AHEAD):
         far_weight(jnp.int32(i), lambda copy: copy.start())
+
+    for copy in small:
+        copy.wait()
 
     down = lax.broadcasted_iota(jnp.int32, (nt, nt), 0)
     across = lax.broadcasted_iota(jnp.int32, (nt, nt), 1)
@@ -206,8 +215,8 @@
 
     def step_d(i):
         j = i % chunks
-        row_copy(i).wait_recv()
-        far_weight(i, lambda copy: copy.wait_recv())
+        row_copy(i).wait()
+        far_weight(i, lambda copy: copy.wait())
 
         @pl.when(i == 0)
         def _():
@@ -282,7 +291,6 @@
 
         @pl.when(i >= chunks)
         def _():
-            out_copy(i).wait_send()
             out_send[j] = grad_rows(j, far).astype(BF16)
             out_copy(i).start()
 
@@ -301,7 +309,7 @@
 
     def step_f(i):
         j = i % chunks
-        out_copy(i).wait_recv()
+        out_copy(i).wait()
         sent_b(j)
 
         @pl.when(i < chunks)
@@ -337,21 +345,27 @@
         @pl.when(i >= chunks)
         def _():
             token_grads[:, columns(j)] = scaled
+            sent_a(j)
+            sent_b(j)
 
     def step_i(i):
         j = i % chunks
 
         @pl.when(i < chunks)
         def _():
-            dwd_copy(i).wait_recv()
+            dwd_copy(i).wait()
             dwd[:, columns(j)] = (mm(hid[0], xg[chunks + j], TN) + dwd_recv[j].astype(F32)).astype(BF16)
 
         @pl.when(i >= chunks)
         def _():
-            dwu_copy(i).wait_recv()
+            dwu_copy(i).wait()
             dwu[columns(j), :] = (mm(xg[j], pg[0], TN) + dwu_recv[j].astype(F32)).astype(BF16)
 
     begin = chunks + LAG_D
+
+    def finish_combine_grads():
+        combine_grads[...] = jnp.sum(
+            jnp.where(eye, jnp.broadcast_to(cg[...], (nt, nt)), 0.0), axis=0, keepdims=True)
 
     def turn(n, _):
         at(n, 0, step_a)
@@ -370,29 +384,11 @@
         at(n, begin + LAG_W, step_w)
         at(n, begin + LAG_G, step_g)
         at(n, begin + LAG_H, step_h)
+        pl.when(n == begin + chunks + LAG_H)(finish_combine_grads)
         at(n, begin + LAG_I, step_i)
         return 0
 
     lax.fori_loop(0, begin + steps + max(LAG_H, LAG_I), turn, 0)
-
-    combine_grads[...] = jnp.sum(jnp.where(eye, jnp.broadcast_to(cg[...], (nt, nt)), 0.0), axis=0, keepdims=True)
-
-    def drain(j, _):
-        sent_a(j)
-        sent_b(j)
-        out_copy(j + chunks).wait_send()
-        dwd_copy(j).wait_send()
-        dwu_copy(j + chunks).wait_send()
-        return 0
-
-    lax.fori_loop(0, chunks, drain, 0)
-
-    def drain_all(i, _):
-        row_copy(i).wait_send()
-        far_weight(i, lambda copy: copy.wait_send())
-        return 0
-
-    lax.fori_loop(0, steps, drain_all, 0)
 
 
 PIECES = 4
@@ -442,13 +438,16 @@
             pltpu.VMEM((width, block), BF16),
             pltpu.VMEM((block, width), BF16),
         ),
-        in_specs=[hbm, hbm, vmem, vmem, vmem, hbm, hbm],
+        in_specs=[hbm] * 7,
         out_specs=(vmem,) * 5,
         scratch_shapes=[
             pltpu.VMEM((nt, width), BF16),
             pltpu.VMEM((nt, width), BF16),
             pltpu.VMEM((width, block), BF16),
             pltpu.VMEM((block, width), BF16),
+            pltpu.VMEM((1, nt), F32),
+            pltpu.VMEM((1, nt), jnp.int32),
+            pltpu.VMEM((2 * slots, 2 * slots), BF16),
             pltpu.VMEM((chunks,) + message, BF16),
             pltpu.VMEM((chunks,) + message, BF16),
             pltpu.VMEM((2 * steps,) + message, BF16),
@@ -476,7 +475,7 @@
             dma((steps,)), dma((steps,)),
             dma((chunks,)), dma((steps,)),
             dma((steps,)), dma((steps,)),
-            dma((steps,)), dma((2,)),
+            dma((steps,)), dma((5,)),
         ],
         compiler_params=pltpu.CompilerParams(
             collective_id=0, has_side_effects=True, vmem_limit_bytes=50 * 1024 * 1024

time: 157 us -> 156 us (level)
  no operation moved by 1% of the time
where the time goes in v3:
time: 156 us; the launch traced here: 155 us
  Pallas kernels  155 us (99%)
    pallas_call x1, Pallas kernels, body(): pl.pallas_call(functools.partial(kernel, side, chunks), out_shape=(pltpu....  151 us
    pallas_call x1, Pallas kernels, body(): pl.pallas_call(hand_over, out_shape=[jax.ShapeDtypeStruct(a.shape, a.dtyp...  3.4 us

profile of v3, /device:TPU:1, one launch (start us, length us, event | category | flops | bytes accessed | tf_op | source)
XLA Modules:
  0.0 155.2 jit_solution(75433421048043750)
XLA Ops:
  0.6 151.2 %shard_map.110 = (bf16[192,3584]{1,0:T(8,128)(2,1)S(1)}, bf16[192,3584]{1,0:T(8,128)(2,1)S(1)}, f32[1,192]{1,0:T(1,128)S(1)}, bf16[3584,256]{1,0:T(8,128)(2,1)S(1)}, bf16[256,3584]{1,0:T(8,128)(2,1)S(1)}) custom-call(bf16[192,3584]{1,0:T(8,128)(2,1)} %tok_hbm.1, bf16[192,3584]{1,0:T(8,128)(2,1)} %cot_hbm.1, f32[1,192]{1,0:T(1,128)} %bitcast.8, ...), custom_call_target="tpu_custom_call" | custom-call | tf_op jit(solution)/shard_map/pallas_call | solution.py:432
  151.8 3.4 %shard_map.111 = (bf16[192,3584]{1,0:T(8,128)(2,1)}, bf16[192,3584]{1,0:T(8,128)(2,1)}, bf16[3584,256]{1,0:T(8,128)(2,1)}, bf16[256,3584]{1,0:T(8,128)(2,1)}, f32[192]{0:T(256)}) custom-call(bf16[192,3584]{1,0:T(8,128)(2,1)S(1)} %get-tuple-element.15.refs_0_, bf16[192,3584]{1,0:T(8,128)(2,1)S(1)} %get-tuple-element.16.refs_1_, ...), custom_call_target="tpu_custom_call" | custom-call | tf_op jit(solution)/shard_map/pallas_call | solution.py:488
